TPU v7x, 32 devices: a whole 2x2x4 slice. The times are simulated.
32 devices in a mesh: groups: 2 (over x), row: 8 (over z, y), col: 2 (over core).
Axes of the slice: x: 2, y: 2, z: 4, core: 2. Of those that a mesh axis runs over, the one named last changes fastest.
Arguments:
- probes: bfloat16 [4, 32, 32768], P(('groups', 'col'), None, 'row'), parts along dimension 0, may hold values from -6 to 6
- tile_data: bfloat16 [16, 2, 96, 256, 256], P(('groups', 'row'), 'col'), parts along dimension 0, may hold values from -0.09375 to 0.09375
- tile_rows: int32 [16, 2, 96], P(('groups', 'row'), 'col'), parts along dimension 0, may hold values from 0 to 7, as said below
- tile_cols: int32 [16, 2, 96], P(('groups', 'row'), 'col'), parts along dimension 0, may hold values from 0 to 127, as said below
- tile_count: int32 [16, 2, 1], P(('groups', 'row'), 'col'), parts along dimension 0, may hold values from 24 to 96, as said below
- active: int32 [32768], P(('groups', 'row')), parts along dimension 0, may hold values 0 or 1
Outputs:
- newton_image: float32 [4, 32, 32768], P(('groups', 'col'), None, 'row'), parts along dimension 0
There are 2 independent parts, one for each index of `groups`. A program takes and returns all parts, laid end to end along the dimension named above; each array names one. Nothing has to cross between parts.
Inputs may be any that keep to these rules, and one draw needn't show every extreme that they name: `tile_rows`: values index a device's 8 row blocks; the (row block, column block) pairs of one device's 96 slots are all distinct. `tile_cols`: values index the 128 column blocks of the device's column group. The live slots of a device are its first tile_count slots; in every part some device has all 96 slots live.
All inputs are finite; a program needn't handle non-finite values. No bound on the sum of `active` on one device may be relied on, other than what follows from the above.
Results may differ from a plain program's by a relative error of at most 0.001.
Values may be sent and summed in bfloat16 or wider, within the bound.
A program may use at most 64 MiB of HBM per device.

v0:
```python
import jax
import jax.numpy as jnp
from jax import lax
from jax.sharding import PartitionSpec as P


def on_device(probes, tile_data, tile_rows, tile_cols, tile_count, active):
    tiles = tile_data[0, 0]
    slot_rows = tile_rows[0, 0]
    slot_cols = tile_cols[0, 0]
    live_count = tile_count[0, 0, 0]
    slot_count = tiles.shape[0]
    tile_size = tiles.shape[1]
    probe_count = probes.shape[1]
    gathered = lax.all_gather(probes[0], "row", axis=1, tiled=True)
    col_blocks = gathered.shape[1] // tile_size
    row_blocks = active.shape[0] // tile_size
    live_slots = jnp.arange(slot_count) < live_count
    row_onehot = (
        (slot_rows[None, :] == jnp.arange(row_blocks)[:, None]) & live_slots[None, :]
    ).astype(jnp.float32)
    col_onehot = (
        (slot_cols[None, :] == jnp.arange(col_blocks)[:, None]) & live_slots[None, :]
    ).astype(jnp.float32)
    picked = gathered.reshape(probe_count, col_blocks, tile_size)[:, slot_cols]
    forward = jnp.einsum("psi,sri->spr", picked, tiles, preferred_element_type=jnp.float32)
    partial_value = jnp.einsum("bs,spr->pbr", row_onehot, forward, precision=lax.Precision.HIGHEST)
    partial_value = partial_value.reshape(probe_count, row_blocks * tile_size)
    row_total = lax.psum(partial_value, "col")
    weighted = (row_total * active.astype(jnp.float32)[None, :]).astype(jnp.bfloat16)
    masked_rows = weighted.reshape(probe_count, row_blocks, tile_size)[:, slot_rows]
    back_terms = jnp.einsum("psr,sri->spi", masked_rows, tiles, preferred_element_type=jnp.float32)
    column_part = jnp.einsum("cs,spi->pci", col_onehot, back_terms, precision=lax.Precision.HIGHEST)
    column_part = column_part.reshape(probe_count, col_blocks * tile_size)
    owned_sum = lax.psum_scatter(column_part, "row", scatter_dimension=1, tiled=True)
    newton_image = probes[0].astype(jnp.float32) + owned_sum
    return newton_image[None]


def solution(mesh):
    placed = (
        P(("groups", "col"), None, "row"),
        P(("groups", "row"), "col", None, None, None),
        P(("groups", "row"), "col", None),
        P(("groups", "row"), "col", None),
        P(("groups", "row"), "col", None),
        P(("groups", "row")),
    )
    return jax.shard_map(
        on_device,
        mesh=mesh,
        in_specs=placed,
        out_specs=P(("groups", "col"), None, "row"),
        check_vma=False,
    )
```

profile of v0, /device:TPU:0, one launch (start us, length us, event | category | flops | bytes accessed | tf_op | source)
XLA Modules:
  0.0 214.2 jit_solution(10062488371197486465)
XLA Ops:
  6.5 0.0 all-gather.3.cloned.1.call-start
  6.5 0.7 all-gather.3.cloned.1.call-update
  7.3 0.0 all-reduce.2.cloned.1.call-start
  7.9 0.7 convert_element_type.12
  8.7 0.7 fusion.24
  9.3 52.2 %all-gather.3.cloned.1.call-done = bf16[1,32,32768]{2,1,0:T(8,128)(2,1)} async-done(((bf16[1,32,4096]{2,1,0:T(8,128)(2,1)}), bf16[1,32,32768]{2,1,0:T(8,128)(2,1)}) %all-gather.3.cloned.1.call-update) | async-done | bytes 2097168 | tf_op jit(solution)/shard_map/all_gather | solution.py:15
  61.5 2.1 copy.14
  63.6 1.2 copy.8
  64.8 1.9 gather_fusion
  66.7 0.0 copy-start.1
  66.7 8.8 %fusion.2 = f32[96,32,256]{2,1,0:T(8,128)S(1)} fusion(bf16[1,1,96,256,256]{4,3,2,1,0:T(8,128)(2,1)} %param.7, bf16[96,32,256]{2,1,0:T(8,128)(2,1)} %gather_fusion), kind=kOutput, calls=%fused_computation.4 | convolution fusion | flops 402653184 | bytes 17301504 | tf_op jit(solution)/shard_map/psi,sri->spr/dot_general | solution.py:26
  75.5 0.0 copy-done.1
  75.6 2.9 %fusion.6 = f32[32,256,8]{1,2,0:T(8,128)S(1)} fusion(f32[96,32,256]{2,1,0:T(8,128)S(1)} %fusion.2, s32[96]{0:T(128)S(1)} %bitcast.57, pred[96]{0:T(512)(128)(4,1)S(1)} %iota_compare_fusion.2), kind=kOutput, calls=%fused_computation.8 | convolution fusion | flops 75499008 | bytes 3408352 | tf_op jit(solution)/shard_map/bs,spr->pbr/dot_general | solution.py:27
  78.5 0.8 copy.15
  79.3 0.0 all-reduce.2.cloned.1.call-update
  79.3 0.0 reduce-scatter.2.cloned.1.call-start
  79.4 16.8 %all-reduce.2.cloned.1.call-done = f32[32,2048]{1,0:T(8,128)} async-done(((f32[32,2048]{1,0:T(8,128)}), f32[32,2048]{1,0:T(8,128)}) %all-reduce.2.cloned.1.call-update) | async-done | bytes 262160 | tf_op jit(solution)/shard_map/psum | solution.py:29
  96.2 1.0 multiply_convert_fusion
  97.2 0.7 gather_fusion.1
  97.9 0.0 copy-start.2
  97.9 6.8 %fusion = f32[96,32,256]{2,1,0:T(8,128)S(1)} fusion(bf16[1,1,96,256,256]{4,3,2,1,0:T(8,128)(2,1)} %param.7, bf16[96,32,256]{2,1,0:T(8,128)(2,1)S(1)} %gather_fusion.1), kind=kOutput, calls=%fused_computation.2 | convolution fusion | flops 402653184 | bytes 17301504 | tf_op jit(solution)/shard_map/psr,sri->spi/dot_general | solution.py:32
  104.7 0.0 copy-done.2
  104.8 6.0 %fusion.8 = f32[32,128,256]{1,2,0:T(8,128)} fusion(f32[96,32,256]{2,1,0:T(8,128)S(1)} %fusion, s32[96]{0:T(128)S(1)} %bitcast.58, pred[96]{0:T(512)(128)(4,1)S(1)} %iota_compare_fusion.2), kind=kOutput, calls=%fused_computation.10 | convolution fusion | flops 1207984128 | bytes 7340512 | tf_op jit(solution)/shard_map/cs,spi->pci/dot_general | solution.py:33
  110.8 5.4 %copy.16 = f32[4,8,128,256]{3,1,2,0:T(8,128)} copy(f32[4,8,128,256]{2,3,1,0:T(8,128)} %bitcast.51) | data formatting | bytes 8388608
  116.2 0.0 copy-start
  116.2 0.0 reduce-scatter.2.cloned.1.call-update
  116.2 89.6 %reduce-scatter.2.cloned.1.call-done = f32[32,4096]{1,0:T(8,128)} async-done(((f32[32,32768]{1,0:T(8,128)}), f32[32,4096]{1,0:T(8,128)}) %reduce-scatter.2.cloned.1.call-update) | async-done | bytes 524304 | tf_op jit(solution)/shard_map/reduce_scatter | solution.py:35
  205.8 0.0 copy-done
  205.8 1.9 fusion.13
  (5 shorter events, 0.0 us)
Async XLA Ops:
  6.5 55.0 %all-gather.3.cloned.1.call-start = ((), (), s32[]{:S(2)}) async-start(), calls=%async_computation.3 | async-start | bytes 2359296 | tf_op jit(solution)/shard_map/all_gather | solution.py:15
  7.3 88.9 %all-reduce.2.cloned.1.call-start = ((), (), s32[]{:S(2)}) async-start(), calls=%async_computation.1 | async-start | bytes 524288 | tf_op jit(solution)/shard_map/psum | solution.py:29
  66.7 8.8 %copy-start.1 = (s32[1,1,96]{2,1,0:T(1,128)S(1)}, s32[1,1,96]{2,1,0:T(1,128)}, u32[]{:S(2)}) copy-start(s32[1,1,96]{2,1,0:T(1,128)} %param.8) | copy-start | bytes 1156
  79.3 126.6 %reduce-scatter.2.cloned.1.call-start = ((), (), s32[]{:S(2)}) async-start(), calls=%async_computation.2 | async-start | bytes 4718592 | tf_op jit(solution)/shard_map/reduce_scatter | solution.py:35
  97.9 6.9 %copy-start.2 = (s32[1,1,96]{2,1,0:T(1,128)S(1)}, s32[1,1,96]{2,1,0:T(1,128)}, u32[]{:S(2)}) copy-start(s32[1,1,96]{2,1,0:T(1,128)} %param.9) | copy-start | bytes 1156
  116.2 89.6 %copy-start = (bf16[1,32,4096]{2,1,0:T(8,128)(2,1)S(1)}, bf16[1,32,4096]{2,1,0:T(8,128)(2,1)}, u32[]{:S(2)}) copy-start(bf16[1,32,4096]{2,1,0:T(8,128)(2,1)} %param.6) | copy-start | bytes 786436
Sparse Core Ops, SparseCore 0:
  9.5 51.9 all-gather.2
  79.4 16.7 all-reduce.1
  116.4 89.4 reduce-scatter.1
where the time goes:
time: 215 us; the launch traced here: 214 us
  waiting for transfers between devices  159 us (74%)
  matrix products  24.6 us (11%)
  between operations  13.8 us (6%)
  local copies, waits for them, and re-layouts  12.2 us (6%)
  other arithmetic  4.23 us (2%)
    reduce_scatter x1, waiting for transfers between devices, on_device(): lax.psum_scatter(column_part, 'row', scatter_dimension=1, tiled=True)  89.6 us
    all_gather x1, waiting for transfers between devices, on_device(): gathered = lax.all_gather(probes[0], 'row', axis=1, tiled=True)  52.2 us
    psum x1, waiting for transfers between devices, on_device(): row_total = lax.psum(partial_value, 'col')  16.8 us
    dot_general x1, matrix products, on_device(): jnp.einsum('psi,sri->spr', picked, tiles, preferred_element_type=jnp.floa...  8.81 us
    unnamed x9, local copies, waits for them, and re-layouts  8.34 us
    dot_general x1, matrix products, on_device(): jnp.einsum('psr,sri->spi', masked_rows, tiles, preferred_element_type=jnp...  6.84 us
    dot_general x1, matrix products, on_device(): jnp.einsum('cs,spi->pci', col_onehot, back_terms, precision=lax.Precision...  6.01 us
  transfers between devices with their start and end apart: 3, of which 3 were waited for; matrix products, arithmetic and copies ran while one was open for 1% of the time, Pallas kernels for 0%

commit v1 on v0

v1 whole, which is shorter than its diff:
```python
import functools

import jax
import jax.numpy as jnp
from jax import lax
from jax.experimental import pallas as pl
from jax.experimental.pallas import tpu as pltpu
from jax.sharding import PartitionSpec as P

MESH = pl.DeviceIdType.MESH
LEVELS = 32000.0
STEPS = 256.0
TINY = 1e-30


def combine(table_ref, terms, dest, blocks, row_blocks, out):
    def body(j, peak):
        first = (dest * blocks + j) * row_blocks
        total = terms[table_ref[first]]
        for k in range(1, row_blocks):
            total = total + terms[table_ref[first + k]]
        out[j] = total
        return jnp.maximum(peak, jnp.abs(total))

    return lax.fori_loop(0, blocks, body, jnp.zeros(out.shape[1:], jnp.float32))


def encode(values, peak, message, blocks):
    half = message.shape[2]
    largest = jnp.max(peak, axis=1, keepdims=True)
    largest = jnp.broadcast_to(largest, (peak.shape[0], half))
    level = jnp.ceil(jnp.log2(jnp.maximum(largest, TINY)) * STEPS)
    scale = LEVELS * jnp.exp2(level * (-1.0 / STEPS))
    message[2 * blocks] = level.astype(jnp.int32).astype(jnp.int16)

    def body(j, carry):
        for h in range(2):
            scaled = jnp.round(values[j, :, h * half : (h + 1) * half] * scale)
            message[2 * j + h] = scaled.astype(jnp.int32).astype(jnp.int16)
        return carry

    lax.fori_loop(0, blocks, body, 0)


def unit(message, blocks):
    level = message[2 * blocks].astype(jnp.int32).astype(jnp.float32)
    return jnp.exp2(level * (1.0 / STEPS)) * (1.0 / LEVELS)


def decoded(message, j, h, scale):
    return message[2 * j + h].astype(jnp.int32).astype(jnp.float32) * scale


def kernel(
    lines, row_blocks, blocks, chunks, unroll,
    cols_ref, rows_ref, mask_ref, table_ref, probes_ref, active_ref, tiles_hbm,
    out_ref,
    tiles, gathered, forward, forward_in, weighted, terms, spare, own,
    y_out, y_in, z_out, z_in,
    tile_sem, up_sem, down_sem, over_sem, gather_sem,
    swap_send, swap_recv, y_send, y_recv, z_send, z_recv,
):
    slots, ts = tiles.shape[0], tiles.shape[1]
    probes = gathered.shape[1]
    half = ts // 2
    me = lax.axis_index("row")
    z, y = me // 2, me % 2
    side = lax.axis_index("col")
    above = jnp.minimum(z + 1, lines - 1) * 2 + y
    below = jnp.maximum(z - 1, 0) * 2 + y
    over = z * 2 + 1 - y
    has_above = z < lines - 1
    has_below = z > 0

    per_chunk = slots // chunks

    def tile_copy(i):
        part = pl.ds(i * per_chunk, per_chunk)
        return pltpu.make_async_copy(tiles_hbm.at[part], tiles.at[part], tile_sem.at[i])

    for i in range(chunks):
        tile_copy(i).start()

    barrier = pltpu.get_barrier_semaphore()
    pl.semaphore_signal(barrier, inc=1, device_id={"row": over}, device_id_type=MESH)
    pl.semaphore_signal(barrier, inc=1, device_id={"col": 1 - side}, device_id_type=MESH)

    @pl.when(has_above)
    def _():
        pl.semaphore_signal(barrier, inc=1, device_id={"row": above}, device_id_type=MESH)

    @pl.when(has_below)
    def _():
        pl.semaphore_signal(barrier, inc=1, device_id={"row": below}, device_id_type=MESH)

    for j in range(blocks):
        gathered[me * blocks + j] = probes_ref[:, j * ts : (j + 1) * ts]
    terms[slots] = jnp.zeros((probes, ts), jnp.float32)

    pl.semaphore_wait(barrier, 2 + jnp.where(has_above, 1, 0) + jnp.where(has_below, 1, 0))

    def shard_copy(r, sem, k, target):
        part = pl.ds(r * blocks, blocks)
        return pltpu.make_async_remote_copy(
            src_ref=gathered.at[part], dst_ref=gathered.at[part],
            send_sem=sem.at[k], recv_sem=gather_sem.at[r],
            device_id={"row": target}, device_id_type=MESH,
        )

    def pass_on(line, go_up, go_down):
        r = line * 2 + y

        @pl.when(go_up)
        def _():
            shard_copy(r, up_sem, line, above).start()

        @pl.when(go_down)
        def _():
            shard_copy(r, down_sem, line, below).start()

        shard_copy(r, over_sem, line, over).start()

    pass_on(z, has_above, has_below)

    def gather_step(k, carry):
        @pl.when(z >= k)
        def _():
            shard_copy((z - k) * 2 + y, up_sem, z - k, over).wait_recv()
            pass_on(z - k, has_above, False)

        @pl.when(z + k < lines)
        def _():
            shard_copy((z + k) * 2 + y, down_sem, z + k, over).wait_recv()
            pass_on(z + k, False, has_below)

        return carry

    lax.fori_loop(1, lines, gather_step, 0)

    def gather_end(line, carry):
        shard_copy(line * 2 + 1 - y, over_sem, line, over).wait_recv()
        shard_copy(line * 2 + y, over_sem, line, over).wait_send()

        @pl.when(has_above & (line <= z))
        def _():
            shard_copy(line * 2 + y, up_sem, line, above).wait_send()

        @pl.when(has_below & (line >= z))
        def _():
            shard_copy(line * 2 + y, down_sem, line, below).wait_send()

        return carry

    lax.fori_loop(0, lines, gather_end, 0)
    for i in range(chunks):
        tile_copy(i).wait()

    forward[...] = jnp.zeros_like(forward)

    def forward_step(i, carry):
        total = None
        for u in range(unroll):
            s = i * unroll + u
            x = gathered[cols_ref[s]]
            spread = jnp.concatenate(
                [
                    x * jnp.full(x.shape, mask_ref[s * row_blocks + b], jnp.float32).astype(x.dtype)
                    for b in range(row_blocks)
                ],
                axis=0,
            )
            product = lax.dot_general(
                spread, tiles[s], (((1,), (1,)), ((), ())), preferred_element_type=jnp.float32
            )
            total = product if total is None else total + product
        forward[...] += total
        return carry

    lax.fori_loop(0, slots // unroll, forward_step, 0)

    swap = pltpu.make_async_remote_copy(
        src_ref=forward, dst_ref=forward_in, send_sem=swap_send, recv_sem=swap_recv,
        device_id={"col": 1 - side}, device_id_type=MESH,
    )
    swap.start()
    swap.wait()
    for b in range(row_blocks):
        part = slice(b * probes, (b + 1) * probes)
        row_sum = forward[part] + forward_in[part]
        weighted[b] = (row_sum * active_ref[b]).astype(weighted.dtype)

    def back_step(i, carry):
        for u in range(unroll):
            s = i * unroll + u
            terms[s] = jnp.dot(
                weighted[rows_ref[s]], tiles[s], preferred_element_type=jnp.float32
            )
        return carry

    lax.fori_loop(0, slots // unroll, back_step, 0)

    def y_copy(line):
        return pltpu.make_async_remote_copy(
            src_ref=y_out.at[line], dst_ref=y_in.at[line],
            send_sem=y_send.at[line], recv_sem=y_recv.at[line],
            device_id={"row": over}, device_id_type=MESH,
        )

    def y_start(line):
        peak = combine(table_ref, terms, line * 2 + 1 - y, blocks, row_blocks, spare)
        encode(spare, peak, y_out.at[line], blocks)
        y_copy(line).start()

    def y_step(i, carry):
        k = lines - 1 - i

        @pl.when(z >= k)
        def _():
            y_start(z - k)

        @pl.when(z + k < lines)
        def _():
            y_start(z + k)

        return carry

    lax.fori_loop(0, lines - 1, y_step, 0)
    y_start(z)

    def own_step(line, carry):
        combine(table_ref, terms, line * 2 + y, blocks, row_blocks, own.at[line])
        return carry

    lax.fori_loop(0, lines, own_step, 0)

    def z_copy(line, slot, target):
        return pltpu.make_async_remote_copy(
            src_ref=z_out.at[line], dst_ref=z_in.at[slot],
            send_sem=z_send.at[line], recv_sem=z_recv.at[slot],
            device_id={"row": target}, device_id_type=MESH,
        )

    def add_in(total, message):
        scale = unit(message, blocks)

        def body(j, peak):
            sums = []
            for h in range(2):
                lanes = slice(h * half, (h + 1) * half)
                value = total[j, :, lanes] + decoded(message, j, h, scale)
                total[j, :, lanes] = value
                sums.append(jnp.abs(value))
            return jnp.maximum(peak, jnp.maximum(*sums))

        return lax.fori_loop(0, blocks, body, jnp.zeros((probes, half), jnp.float32))

    def z_start(line, upstream, slot, target):
        y_copy(line).wait_recv()
        peak = add_in(own.at[line], y_in.at[line])
        spare_peak[...] = peak

        @pl.when(upstream)
        def _():
            z_copy(line, line, target).wait_recv()
            spare_peak[...] = add_in(own.at[line], z_in.at[line])

        encode(own.at[line], spare_peak[...], z_out.at[line], blocks)
        z_copy(line, slot, target).start()

    spare_peak = spare.at[0, :, pl.ds(0, half)]

    def z_step(i, carry):
        k = lines - 1 - i

        @pl.when(z >= k)
        def _():
            z_start(z - k, has_above, jnp.where(k == 1, lines, z - k), below)

        @pl.when(z + k < lines)
        def _():
            z_start(z + k, has_below, z + k, above)

        return carry

    lax.fori_loop(0, lines - 1, z_step, 0)

    total = own.at[z]
    y_copy(z).wait_recv()
    add_in(total, y_in.at[z])

    @pl.when(has_below)
    def _():
        z_copy(z, z, below).wait_recv()
        add_in(total, z_in.at[z])

    @pl.when(has_above)
    def _():
        z_copy(z, lines, above).wait_recv()
        add_in(total, z_in.at[lines])

    for j in range(blocks):
        out_ref[:, j * ts : (j + 1) * ts] = total[j]

    def z_end(line, carry):
        y_copy(line).wait_send()

        @pl.when(line != z)
        def _():
            z_copy(line, line, over).wait_send()

        return carry

    lax.fori_loop(0, lines, z_end, 0)


def on_device(row_devices, probes, tile_data, tile_rows, tile_cols, tile_count, active):
    tiles = tile_data[0, 0]
    slot_rows = tile_rows[0, 0]
    slot_cols = tile_cols[0, 0]
    live_count = tile_count[0, 0, 0]
    slots, ts = tiles.shape[0], tiles.shape[1]
    probe_count, owned = probes.shape[1], probes.shape[2]
    blocks = owned // ts
    col_blocks = row_devices * blocks
    row_blocks = active.shape[0] // ts
    lines = row_devices // 2
    chunks = 8 if slots % 8 == 0 else 1
    unroll = 4 if slots % 4 == 0 else 1

    index = jnp.arange(slots, dtype=jnp.int32)
    live = index < live_count
    mask = (slot_rows[:, None] == jnp.arange(row_blocks)[None, :]) & live[:, None]
    mask = mask.astype(jnp.float32).reshape(-1)
    pair = jnp.where(live, slot_cols * row_blocks + slot_rows, -1)
    place = jnp.arange(col_blocks * row_blocks, dtype=jnp.int32)
    table = jnp.min(jnp.where(place[:, None] == pair[None, :], index[None, :], slots), axis=1)

    smem = pl.BlockSpec(memory_space=pltpu.SMEM)
    vmem = pl.BlockSpec(memory_space=pltpu.VMEM)
    f32, bf16, dma = jnp.float32, jnp.bfloat16, pltpu.SemaphoreType.DMA
    message = (2 * blocks + 1, probe_count, ts // 2)
    back = pl.pallas_call(
        functools.partial(kernel, lines, row_blocks, blocks, chunks, unroll),
        out_shape=jax.ShapeDtypeStruct((probe_count, owned), f32),
        in_specs=[smem, smem, smem, smem, vmem, vmem, pl.BlockSpec(memory_space=pl.ANY)],
        out_specs=vmem,
        scratch_shapes=[
            pltpu.VMEM(tiles.shape, bf16),
            pltpu.VMEM((col_blocks, probe_count, ts), bf16),
            pltpu.VMEM((row_blocks * probe_count, ts), f32),
            pltpu.VMEM((row_blocks * probe_count, ts), f32),
            pltpu.VMEM((row_blocks, probe_count, ts), bf16),
            pltpu.VMEM((slots + 1, probe_count, ts), f32),
            pltpu.VMEM((blocks, probe_count, ts), f32),
            pltpu.VMEM((lines, blocks, probe_count, ts), f32),
            pltpu.VMEM((lines,) + message, jnp.int16),
            pltpu.VMEM((lines,) + message, jnp.int16),
            pltpu.VMEM((lines,) + message, jnp.int16),
            pltpu.VMEM((lines + 1,) + message, jnp.int16),
            dma((chunks,)), dma((lines,)), dma((lines,)), dma((lines,)), dma((row_devices,)),
            dma, dma, dma((lines,)), dma((lines,)), dma((lines,)), dma((lines + 1,)),
        ],
        compiler_params=pltpu.CompilerParams(
            collective_id=0, has_side_effects=True, vmem_limit_bytes=56 * 1024 * 1024
        ),
        cost_estimate=pl.CostEstimate(
            flops=2 * slots * ts * ts * probe_count * (row_blocks + 1),
            bytes_accessed=2 * tiles.size, transcendentals=0,
        ),
    )(
        slot_cols, slot_rows, mask, table,
        probes[0], active.astype(f32).reshape(row_blocks, 1, ts), tiles,
    )
    return (probes[0].astype(f32) + back)[None]


def solution(mesh):
    placed = (
        P(("groups", "col"), None, "row"),
        P(("groups", "row"), "col", None, None, None),
        P(("groups", "row"), "col", None),
        P(("groups", "row"), "col", None),
        P(("groups", "row"), "col", None),
        P(("groups", "row")),
    )
    return jax.shard_map(
        functools.partial(on_device, mesh.shape["row"]),
        mesh=mesh,
        in_specs=placed,
        out_specs=P(("groups", "col"), None, "row"),
        check_vma=False,
    )
```

time: 215 us -> 82 us (0.38)
  waiting for transfers between devices: 159 us -> 0 us
  Pallas kernels: 0 us -> 75 us
  matrix products: 24.6 us -> 0 us
  between operations: 13.8 us -> 0.72 us
  local copies, waits for them, and re-layouts: 12.2 us -> 0.68 us
    reduce_scatter x1 -> x0, waiting for transfers between devices: 89.6 us -> none  [on_device(): lax.psum_scatter(column_part, 'row', scatter_dimension=1, tiled=True)]
    pallas_call x0 -> x1, Pallas kernels: none -> 75 us  [on_device(): pl.pallas_call(functools.partial(kernel, lines, row_blocks, blocks, chunk...]
    all_gather x1 -> x0, waiting for transfers between devices: 52.2 us -> none  [on_device(): gathered = lax.all_gather(probes[0], 'row', axis=1, tiled=True)]
    dot_general x4 -> x0, matrix products: 24.6 us -> none  [the longest x1 8.81 us: on_device(): jnp.einsum('psi,sri->spr', picked, tiles, preferred_element_type=jnp.floa...]
    psum x1 -> x0, waiting for transfers between devices: 16.8 us -> none  [on_device(): row_total = lax.psum(partial_value, 'col')]
    unnamed x9 -> x2, local copies, waits for them, and re-layouts: 8.34 us -> 0.01 us
    gather x2 -> x0, local copies, waits for them, and re-layouts: 2.62 us -> none  [the longest x1 1.91 us: on_device(): picked = gathered.reshape(probe_count, col_blocks, tile_size)[:, slot_cols]]
  transfers between devices with their start and end apart: 3 -> 0, of which waited for: 3 -> 0; matrix products, arithmetic and copies ran while one was open for 1% -> 0% of each run, Pallas kernels for 0% -> 0%
where the time goes in v1:
time: 82 us; the launch traced here: 81.8 us
  Pallas kernels  75 us (91%)
  other arithmetic  5.31 us (6%)
    pallas_call x1, Pallas kernels, on_device(): pl.pallas_call(functools.partial(kernel, lines, row_blocks, blocks, chunk...  75 us
    broadcast_in_dim x1, other arithmetic, on_device(): return (probes[0].astype(f32) + back)[None]  1.88 us

profile of v1, /device:TPU:0, one launch (start us, length us, event | category | flops | bytes accessed | tf_op | source)
XLA Modules:
  0.0 81.8 jit_solution(17990307727536807185)
XLA Ops:
  0.0 0.0 copy-start
  0.7 0.7 add_select_fusion
  1.4 0.7 select_reduce_fusion.table_ref
  2.1 1.3 %convert_element_type.16 = f32[2048]{0:T(1024)} convert(s32[2048]{0:T(1024)} %param.11) | non-fusion elementwise | flops 2048 | bytes 16384 | tf_op jit(solution)/shard_map/convert_element_type | solution.py:372
  3.4 0.7 fusion.1
  4.1 0.7 reshape.32.mask_ref
  4.8 75.0 %shard_map.64 = f32[32,4096]{1,0:T(8,128)} custom-call(s32[96]{0:T(128)} %bitcast.17, s32[96]{0:T(128)} %bitcast.16, f32[768]{0:T(1024)} %reshape.32.mask_ref, s32[1024]{0:T(1024)} %select_reduce_fusion.table_ref, bf16[32,4096]{1,0:T(8,128)(2,1)} %bitcast.13, f32[8,1,256]{2,1,0:T(1,128)} %bitcast.14, bf16[96,256,256]{2,1,0:T(8,128)(2,1)} %bitcast.18), custom_call_target="tpu_custom_call" | custom-call | flops 3623878656 | bytes 12582912 | tf_op jit(solution)/shard_map/pallas_call | solution.py:342
  79.9 0.0 copy-done
  79.9 1.9 %add_bitcast_fusion = f32[1,32,4096]{2,1,0:T(8,128)} fusion(f32[32,4096]{1,0:T(8,128)} %shard_map.64, bf16[1,32,4096]{2,1,0:T(8,128)(2,1)S(1)} %copy-done), kind=kLoop, calls=%fused_computation | loop fusion | flops 262144 | bytes 1310720 | tf_op jit(solution)/shard_map/broadcast_in_dim | solution.py:374
  (1 shorter events, 0.0 us)
Async XLA Ops:
  0.0 79.9 %copy-start = (bf16[1,32,4096]{2,1,0:T(8,128)(2,1)S(1)}, bf16[1,32,4096]{2,1,0:T(8,128)(2,1)}, u32[]{:S(2)}) copy-start(bf16[1,32,4096]{2,1,0:T(8,128)(2,1)} %param.6) | copy-start | bytes 786436

commit v2 on v0

v2 whole, which is shorter than its diff:
```python
import functools

import jax
import jax.numpy as jnp
from jax import lax
from jax.experimental import pallas as pl
from jax.experimental.pallas import tpu as pltpu
from jax.sharding import PartitionSpec as P

MESH = pl.DeviceIdType.MESH
LEVELS = 32000.0
STEPS = 256.0
TINY = 1e-30


def over_blocks(blocks, body, start):
    step = 4 if blocks % 4 == 0 else 1

    def several(i, carry):
        for u in range(step):
            carry = body(i * step + u, carry)
        return carry

    return lax.fori_loop(0, blocks // step, several, start)


def combine(table_ref, terms, dest, blocks, row_blocks, out):
    def body(j, peak):
        col = dest * blocks + j
        total = terms[table_ref[0, col]]
        for k in range(1, row_blocks):
            total = total + terms[table_ref[k, col]]
        out[j] = total
        return jnp.maximum(peak, jnp.abs(total))

    return over_blocks(blocks, body, jnp.zeros(out.shape[1:], jnp.float32))


def encode(values, peak, message, blocks):
    half = message.shape[2]
    largest = jnp.max(peak, axis=1, keepdims=True)
    largest = jnp.broadcast_to(largest, (peak.shape[0], half))
    level = jnp.ceil(jnp.log2(jnp.maximum(largest, TINY)) * STEPS)
    scale = LEVELS * jnp.exp2(level * (-1.0 / STEPS))
    message[2 * blocks] = level.astype(jnp.int32).astype(jnp.int16)

    def body(j, carry):
        for h in range(2):
            scaled = jnp.round(values[j, :, h * half : (h + 1) * half] * scale)
            message[2 * j + h] = scaled.astype(jnp.int32).astype(jnp.int16)
        return carry

    over_blocks(blocks, body, 0)


def unit(message, blocks):
    level = message[2 * blocks].astype(jnp.int32).astype(jnp.float32)
    return jnp.exp2(level * (1.0 / STEPS)) * (1.0 / LEVELS)


def decoded(message, j, h, scale):
    return message[2 * j + h].astype(jnp.int32).astype(jnp.float32) * scale


def kernel(
    lines, row_blocks, blocks, chunks, unroll, parts,
    cols_ref, rows_ref, count_ref, probes_ref, active_ref, tiles_hbm,
    out_ref,
    tiles, turned, gathered_first, gathered_second, forward, forward_in, weighted, terms, spare, own,
    y_out, y_in, z_out, z_in, table_vmem, table_ref,
    tile_sem, table_sem, up_sem, down_sem, over_sem, gather_sem,
    swap_send, swap_recv, y_send, y_recv, z_send, z_recv,
):
    slots, ts = tiles.shape[0], tiles.shape[1]
    gathered = (gathered_first, gathered_second)
    probes = gathered_first.shape[1]
    half = ts // 2
    me = lax.axis_index("row")
    z, y = me // 2, me % 2
    side = lax.axis_index("col")
    above = jnp.minimum(z + 1, lines - 1) * 2 + y
    below = jnp.maximum(z - 1, 0) * 2 + y
    over = z * 2 + 1 - y
    has_above = z < lines - 1
    has_below = z > 0

    per_chunk = slots // chunks

    def tile_copy(i):
        part = pl.ds(i * per_chunk, per_chunk)
        return pltpu.make_async_copy(tiles_hbm.at[part], tiles.at[part], tile_sem.at[i])

    barrier = pltpu.get_barrier_semaphore()
    pl.semaphore_signal(barrier, inc=1, device_id={"row": over}, device_id_type=MESH)
    pl.semaphore_signal(barrier, inc=1, device_id={"col": 1 - side}, device_id_type=MESH)

    @pl.when(has_above)
    def _():
        pl.semaphore_signal(barrier, inc=1, device_id={"row": above}, device_id_type=MESH)

    @pl.when(has_below)
    def _():
        pl.semaphore_signal(barrier, inc=1, device_id={"row": below}, device_id_type=MESH)

    for i in range(chunks):
        tile_copy(i).start()

    for h in range(parts):
        for j in range(blocks):
            gathered[h][me * blocks + j] = probes_ref[
                h * probes : (h + 1) * probes, j * ts : (j + 1) * ts
            ]

    pl.semaphore_wait(barrier, 2 + jnp.where(has_above, 1, 0) + jnp.where(has_below, 1, 0))

    def shard_copy(h, r, sem, k, target):
        part = pl.ds(r * blocks, blocks)
        return pltpu.make_async_remote_copy(
            src_ref=gathered[h].at[part], dst_ref=gathered[h].at[part],
            send_sem=sem.at[h, k], recv_sem=gather_sem.at[h, r],
            device_id={"row": target}, device_id_type=MESH,
        )

    def pass_on(h, line, go_up, go_down):
        r = line * 2 + y

        @pl.when(go_up)
        def _():
            shard_copy(h, r, up_sem, line, above).start()

        @pl.when(go_down)
        def _():
            shard_copy(h, r, down_sem, line, below).start()

        shard_copy(h, r, over_sem, line, over).start()

    def gather_steps(h, first, last):
        def step(k, carry):
            @pl.when(z >= k)
            def _():
                shard_copy(h, (z - k) * 2 + y, up_sem, z - k, over).wait_recv()
                pass_on(h, z - k, has_above, False)

            @pl.when(z + k < lines)
            def _():
                shard_copy(h, (z + k) * 2 + y, down_sem, z + k, over).wait_recv()
                pass_on(h, z + k, False, has_below)

            return carry

        lax.fori_loop(first, last, step, 0)

    def gather_end(h):
        def step(line, carry):
            shard_copy(h, line * 2 + 1 - y, over_sem, line, over).wait_recv()
            shard_copy(h, line * 2 + y, over_sem, line, over).wait_send()

            @pl.when(has_above & (line <= z))
            def _():
                shard_copy(h, line * 2 + y, up_sem, line, above).wait_send()

            @pl.when(has_below & (line >= z))
            def _():
                shard_copy(h, line * 2 + y, down_sem, line, below).wait_send()

            return carry

        lax.fori_loop(0, lines, step, 0)

    def forward_steps(h, first, last):
        def step(i, carry):
            total = None
            for u in range(unroll):
                s = i * unroll + u
                x = gathered[h][cols_ref[0, 0, s]]
                row = jnp.where(s < count_ref[0, 0, 0], rows_ref[0, 0, s], -1)
                spread = jnp.concatenate(
                    [
                        x * jnp.full(x.shape, jnp.where(row == b, 1.0, 0.0), jnp.float32).astype(x.dtype)
                        for b in range(row_blocks)
                    ],
                    axis=0,
                )
                product = jnp.dot(spread, turned[s], preferred_element_type=jnp.float32)
                total = product if total is None else total + product
            forward[h] += total
            return carry

        lax.fori_loop(first, last, step, 0)

    def swap(h):
        return pltpu.make_async_remote_copy(
            src_ref=forward.at[h], dst_ref=forward_in.at[h],
            send_sem=swap_send.at[h], recv_sem=swap_recv.at[h],
            device_id={"col": 1 - side}, device_id_type=MESH,
        )

    def weigh(h):
        for b in range(row_blocks):
            part = slice(b * probes, (b + 1) * probes)
            row_sum = forward[h, part] + forward_in[h, part]
            mask = jnp.concatenate(
                [active_ref[2 * b + i : 2 * b + i + 1, :] for i in range(2)], axis=1
            ).astype(jnp.float32)
            weighted[h, b] = (row_sum * mask).astype(weighted.dtype)

    def back_steps(h, first, last):
        def step(i, carry):
            for u in range(unroll):
                s = i * unroll + u
                terms[h, s] = jnp.dot(
                    weighted[h, rows_ref[0, 0, s]], tiles[s], preferred_element_type=jnp.float32
                )
            return carry

        lax.fori_loop(first, last, step, 0)

    def y_copy(h, line):
        return pltpu.make_async_remote_copy(
            src_ref=y_out.at[h, line], dst_ref=y_in.at[h, line],
            send_sem=y_send.at[h, line], recv_sem=y_recv.at[h, line],
            device_id={"row": over}, device_id_type=MESH,
        )

    def y_start(h, line):
        peak = combine(table_ref, terms.at[h], line * 2 + 1 - y, blocks, row_blocks, spare)
        encode(spare, peak, y_out.at[h, line], blocks)
        y_copy(h, line).start()

    def y_all(h):
        def step(i, carry):
            k = lines - 1 - i

            @pl.when(z >= k)
            def _():
                y_start(h, z - k)

            @pl.when(z + k < lines)
            def _():
                y_start(h, z + k)

            return carry

        lax.fori_loop(0, lines - 1, step, 0)
        y_start(h, z)

        def own_step(line, carry):
            combine(table_ref, terms.at[h], line * 2 + y, blocks, row_blocks, own.at[h, line])
            return carry

        lax.fori_loop(0, lines, own_step, 0)

    def z_copy(h, line, slot, target):
        return pltpu.make_async_remote_copy(
            src_ref=z_out.at[h, line], dst_ref=z_in.at[h, slot],
            send_sem=z_send.at[h, line], recv_sem=z_recv.at[h, slot],
            device_id={"row": target}, device_id_type=MESH,
        )

    def add_in(total, message):
        scale = unit(message, blocks)

        def body(j, peak):
            sums = []
            for i in range(2):
                lanes = slice(i * half, (i + 1) * half)
                value = total[j, :, lanes] + decoded(message, j, i, scale)
                total[j, :, lanes] = value
                sums.append(jnp.abs(value))
            return jnp.maximum(peak, jnp.maximum(*sums))

        return over_blocks(blocks, body, jnp.zeros((probes, half), jnp.float32))

    peak_ref = spare.at[0, :, pl.ds(0, half)]

    def z_start(h, line, upstream, slot, target):
        y_copy(h, line).wait_recv()
        peak_ref[...] = add_in(own.at[h, line], y_in.at[h, line])

        @pl.when(upstream)
        def _():
            z_copy(h, line, line, target).wait_recv()
            peak_ref[...] = add_in(own.at[h, line], z_in.at[h, line])

        encode(own.at[h, line], peak_ref[...], z_out.at[h, line], blocks)
        z_copy(h, line, slot, target).start()

    def z_steps(h, first, last):
        def step(i, carry):
            k = lines - i

            @pl.when(z >= k)
            def _():
                z_start(h, z - k, has_above, jnp.where(k == 1, lines, z - k), below)

            @pl.when(z + k < lines)
            def _():
                z_start(h, z + k, has_below, z + k, above)

            return carry

        lax.fori_loop(first, last, step, 0)

    def finish(h):
        total = own.at[h, z]
        y_copy(h, z).wait_recv()
        add_in(total, y_in.at[h, z])

        @pl.when(has_below)
        def _():
            z_copy(h, z, z, below).wait_recv()
            add_in(total, z_in.at[h, z])

        @pl.when(has_above)
        def _():
            z_copy(h, z, lines, above).wait_recv()
            add_in(total, z_in.at[h, lines])

        for j in range(blocks):
            out_ref[h * probes : (h + 1) * probes, j * ts : (j + 1) * ts] = total[j]

    def z_end(h):
        def step(line, carry):
            y_copy(h, line).wait_send()

            @pl.when(line != z)
            def _():
                z_copy(h, line, line, over).wait_send()

            return carry

        lax.fori_loop(0, lines, step, 0)

    groups = slots // unroll
    middle = groups // 2
    cuts = [1 + (lines - 1) * i // 3 for i in range(4)]

    def compute(h, beside):
        forward_steps(h, 0, middle)
        beside(cuts[0], cuts[1])
        forward_steps(h, middle, groups)
        swap(h).start()
        beside(cuts[1], cuts[2])
        swap(h).wait()
        weigh(h)
        back_steps(h, 0, middle)
        beside(cuts[2], cuts[3])
        back_steps(h, middle, groups)

    pass_on(0, z, has_above, has_below)

    shape = table_vmem.shape
    place = lax.broadcasted_iota(jnp.int32, shape, 1) * row_blocks + lax.broadcasted_iota(jnp.int32, shape, 0)

    def table_step(s, table):
        pair = jnp.where(s < count_ref[0, 0, 0], cols_ref[0, 0, s] * row_blocks + rows_ref[0, 0, s], -1)
        return jnp.where(place == pair, s, table)

    table_vmem[...] = lax.fori_loop(0, slots, table_step, jnp.full(shape, slots, jnp.int32))
    table_copy = pltpu.make_async_copy(table_vmem, table_ref, table_sem)
    table_copy.start()
    for h in range(parts):
        terms[h, slots] = jnp.zeros((probes, ts), jnp.float32)
        forward[h] = jnp.zeros(forward.shape[1:], jnp.float32)

    turns = [1 + min(lines - 1, (lines - 1) * i * 4 // (3 * chunks)) for i in range(chunks + 1)]

    for i in range(chunks):
        tile_copy(i).wait()

        def turn_step(n, carry):
            for u in range(2):
                s = i * per_chunk + n * 2 + u
                turned[s] = tiles[s].T
            return carry

        lax.fori_loop(0, per_chunk // 2, turn_step, 0)
        gather_steps(0, turns[i], turns[i + 1])
        if turns[i] < turns[i + 1] == lines:
            pass_on(1, z, has_above, has_below)
    table_copy.wait()
    gather_end(0)
    for h in range(parts):
        compute(h, functools.partial(gather_steps, 1) if h == 0 else functools.partial(z_steps, 0))
        y_all(h)
        if h == 0:
            gather_end(1)
    finish(0)
    z_steps(1, 1, lines)
    finish(1)
    z_end(0)
    z_end(1)


def on_device(row_devices, probes, tile_data, tile_rows, tile_cols, tile_count, active):
    tiles = tile_data[0, 0]
    slots, ts = tiles.shape[0], tiles.shape[1]
    probe_count, owned = probes.shape[1], probes.shape[2]
    blocks = owned // ts
    col_blocks = row_devices * blocks
    row_blocks = active.shape[0] // ts
    lines = row_devices // 2
    chunks = 8 if slots % 16 == 0 else 1
    unroll = 16 if slots % 16 == 0 else 1
    parts = 2
    share = probe_count // parts

    smem = pl.BlockSpec(memory_space=pltpu.SMEM)
    vmem = pl.BlockSpec(memory_space=pltpu.VMEM)
    f32, bf16, dma = jnp.float32, jnp.bfloat16, pltpu.SemaphoreType.DMA
    message = (2 * blocks + 1, share, ts // 2)
    back = pl.pallas_call(
        functools.partial(kernel, lines, row_blocks, blocks, chunks, unroll, parts),
        out_shape=jax.ShapeDtypeStruct((probe_count, owned), f32),
        in_specs=[smem, smem, smem, vmem, vmem, pl.BlockSpec(memory_space=pl.ANY)],
        out_specs=vmem,
        scratch_shapes=[
            pltpu.VMEM(tiles.shape, bf16),
            pltpu.VMEM(tiles.shape, bf16),
            pltpu.VMEM((col_blocks, share, ts), bf16),
            pltpu.VMEM((col_blocks, share, ts), bf16),
            pltpu.VMEM((parts, row_blocks * share, ts), f32),
            pltpu.VMEM((parts, row_blocks * share, ts), f32),
            pltpu.VMEM((parts, row_blocks, share, ts), bf16),
            pltpu.VMEM((parts, slots + 1, share, ts), f32),
            pltpu.VMEM((blocks, share, ts), f32),
            pltpu.VMEM((parts, lines, blocks, share, ts), f32),
            pltpu.VMEM((parts, lines) + message, jnp.int16),
            pltpu.VMEM((parts, lines) + message, jnp.int16),
            pltpu.VMEM((parts, lines) + message, jnp.int16),
            pltpu.VMEM((parts, lines + 1) + message, jnp.int16),
            pltpu.VMEM((row_blocks, col_blocks), jnp.int32),
            pltpu.SMEM((row_blocks, col_blocks), jnp.int32),
            dma((chunks,)), dma,
            dma((parts, lines)), dma((parts, lines)), dma((parts, lines)), dma((parts, row_devices)),
            dma((parts,)), dma((parts,)),
            dma((parts, lines)), dma((parts, lines)), dma((parts, lines)), dma((parts, lines + 1)),
        ],
        compiler_params=pltpu.CompilerParams(
            collective_id=0, has_side_effects=True, vmem_limit_bytes=56 * 1024 * 1024
        ),
        cost_estimate=pl.CostEstimate(
            flops=2 * slots * ts * ts * probe_count * (row_blocks + 1),
            bytes_accessed=2 * tiles.size, transcendentals=0,
        ),
    )(
        tile_cols, tile_rows, tile_count,
        probes[0], active.reshape(row_blocks * 2, ts // 2), tiles,
    )
    return (probes[0].astype(f32) + back)[None]


def solution(mesh):
    placed = (
        P(("groups", "col"), None, "row"),
        P(("groups", "row"), "col", None, None, None),
        P(("groups", "row"), "col", None),
        P(("groups", "row"), "col", None),
        P(("groups", "row"), "col", None),
        P(("groups", "row")),
    )
    return jax.shard_map(
        functools.partial(on_device, mesh.shape["row"]),
        mesh=mesh,
        in_specs=placed,
        out_specs=P(("groups", "col"), None, "row"),
        check_vma=False,
    )
```

time: 215 us -> 70.7 us (0.33)
  waiting for transfers between devices: 159 us -> 0 us
  Pallas kernels: 0 us -> 68 us
  matrix products: 24.6 us -> 0 us
  between operations: 13.8 us -> 0.71 us
  local copies, waits for them, and re-layouts: 12.2 us -> 0.01 us
  other arithmetic: 4.23 us -> 1.88 us
    reduce_scatter x1 -> x0, waiting for transfers between devices: 89.6 us -> none  [on_device(): lax.psum_scatter(column_part, 'row', scatter_dimension=1, tiled=True)]
    pallas_call x0 -> x1, Pallas kernels: none -> 68 us  [on_device(): pl.pallas_call(functools.partial(kernel, lines, row_blocks, blocks, chunk...]
    all_gather x1 -> x0, waiting for transfers between devices: 52.2 us -> none  [on_device(): gathered = lax.all_gather(probes[0], 'row', axis=1, tiled=True)]
    dot_general x4 -> x0, matrix products: 24.6 us -> none  [the longest x1 8.81 us: on_device(): jnp.einsum('psi,sri->spr', picked, tiles, preferred_element_type=jnp.floa...]
    psum x1 -> x0, waiting for transfers between devices: 16.8 us -> none  [on_device(): row_total = lax.psum(partial_value, 'col')]
    unnamed x9 -> x2, local copies, waits for them, and re-layouts: 8.34 us -> 0.01 us
    gather x2 -> x0, local copies, waits for them, and re-layouts: 2.62 us -> none  [the longest x1 1.91 us: on_device(): picked = gathered.reshape(probe_count, col_blocks, tile_size)[:, slot_cols]]
  transfers between devices with their start and end apart: 3 -> 0, of which waited for: 3 -> 0; matrix products, arithmetic and copies ran while one was open for 1% -> 0% of each run, Pallas kernels for 0% -> 0%
where the time goes in v2:
time: 70.7 us; the launch traced here: 70.6 us
  Pallas kernels  68 us (96%)
  other arithmetic  1.88 us (3%)
  between operations  0.71 us (1%)
    pallas_call x1, Pallas kernels, on_device(): pl.pallas_call(functools.partial(kernel, lines, row_blocks, blocks, chunk...  68 us
    broadcast_in_dim x1, other arithmetic, on_device(): return (probes[0].astype(f32) + back)[None]  1.88 us

profile of v2, /device:TPU:0, one launch (start us, length us, event | category | flops | bytes accessed | tf_op | source)
XLA Modules:
  0.0 70.6 jit_solution(1104396450458871936)
XLA Ops:
  0.0 0.0 copy-start
  0.7 68.0 %shard_map.64 = f32[32,4096]{1,0:T(8,128)} custom-call(s32[1,1,96]{2,1,0:T(1,128)} %cols_ref.1, s32[1,1,96]{2,1,0:T(1,128)} %rows_ref.1, s32[1,1,1]{2,1,0:T(1,128)S(6)} %copy.7.count_ref, bf16[32,4096]{1,0:T(8,128)(2,1)} %bitcast.6, s32[16,128]{1,0:T(8,128)} %bitcast.8, bf16[96,256,256]{2,1,0:T(8,128)(2,1)} %bitcast.7), custom_call_target="tpu_custom_call" | custom-call | flops 3623878656 | bytes 12582912 | tf_op jit(solution)/shard_map/pallas_call | solution.py:412
  68.7 0.0 copy-done
  68.7 1.9 %add_bitcast_fusion = f32[1,32,4096]{2,1,0:T(8,128)} fusion(f32[32,4096]{1,0:T(8,128)} %shard_map.64, bf16[1,32,4096]{2,1,0:T(8,128)(2,1)S(1)} %copy-done), kind=kLoop, calls=%fused_computation | loop fusion | flops 262144 | bytes 1310720 | tf_op jit(solution)/shard_map/broadcast_in_dim | solution.py:450
Async XLA Ops:
  0.0 68.7 %copy-start = (bf16[1,32,4096]{2,1,0:T(8,128)(2,1)S(1)}, bf16[1,32,4096]{2,1,0:T(8,128)(2,1)}, u32[]{:S(2)}) copy-start(bf16[1,32,4096]{2,1,0:T(8,128)(2,1)} %param.6) | copy-start | bytes 786436

commit v3 on v2

--- a/solution.py
+++ b/solution.py
@@ -381,12 +381,14 @@
     table_copy.wait()
     gather_end(0)
     for h in range(parts):
-        compute(h, functools.partial(gather_steps, 1) if h == 0 else functools.partial(z_steps, 0))
+        compute(h, functools.partial(gather_steps, 1) if h == 0 else lambda first, last: None)
         y_all(h)
         if h == 0:
             gather_end(1)
+    for i in range(3):
+        z_steps(0, cuts[i], cuts[i + 1])
+        z_steps(1, cuts[i], cuts[i + 1])
     finish(0)
-    z_steps(1, 1, lines)
     finish(1)
     z_end(0)
     z_end(1)

time: 70.7 us -> 67 us (0.948)
  Pallas kernels: 68 us -> 64.2 us
    pallas_call x1, Pallas kernels: 68 us -> 64.2 us  [on_device(): pl.pallas_call(functools.partial(kernel, lines, row_blocks, blocks, chunk...]
where the time goes in v3:
time: 67 us; the launch traced here: 66.8 us
  Pallas kernels  64.2 us (96%)
  other arithmetic  1.88 us (3%)
  between operations  0.71 us (1%)
    pallas_call x1, Pallas kernels, on_device(): pl.pallas_call(functools.partial(kernel, lines, row_blocks, blocks, chunk...  64.2 us
    broadcast_in_dim x1, other arithmetic, on_device(): return (probes[0].astype(f32) + back)[None]  1.88 us

profile of v3, /device:TPU:0, one launch (start us, length us, event | category | flops | bytes accessed | tf_op | source)
XLA Modules:
  0.0 66.8 jit_solution(12563521197117405075)
XLA Ops:
  0.0 0.0 copy-start
  0.7 64.2 %shard_map.64 = f32[32,4096]{1,0:T(8,128)} custom-call(s32[1,1,96]{2,1,0:T(1,128)} %cols_ref.1, s32[1,1,96]{2,1,0:T(1,128)} %rows_ref.1, s32[1,1,1]{2,1,0:T(1,128)S(6)} %copy.7.count_ref, bf16[32,4096]{1,0:T(8,128)(2,1)} %bitcast.6, s32[16,128]{1,0:T(8,128)} %bitcast.8, bf16[96,256,256]{2,1,0:T(8,128)(2,1)} %bitcast.7), custom_call_target="tpu_custom_call" | custom-call | flops 3623878656 | bytes 12582912 | tf_op jit(solution)/shard_map/pallas_call | solution.py:414
  64.9 0.0 copy-done
  64.9 1.9 %add_bitcast_fusion = f32[1,32,4096]{2,1,0:T(8,128)} fusion(f32[32,4096]{1,0:T(8,128)} %shard_map.64, bf16[1,32,4096]{2,1,0:T(8,128)(2,1)S(1)} %copy-done), kind=kLoop, calls=%fused_computation | loop fusion | flops 262144 | bytes 1310720 | tf_op jit(solution)/shard_map/broadcast_in_dim | solution.py:452
Async XLA Ops:
  0.0 64.9 %copy-start = (bf16[1,32,4096]{2,1,0:T(8,128)(2,1)S(1)}, bf16[1,32,4096]{2,1,0:T(8,128)(2,1)}, u32[]{:S(2)}) copy-start(bf16[1,32,4096]{2,1,0:T(8,128)(2,1)} %param.6) | copy-start | bytes 786436
